TPU v7x, 32 devices: a whole 2x2x4 slice. The times are simulated.
32 devices in a mesh: groups: 2 (over y), ctx: 4 (over x, core), head: 4 (over z).
Axes of the slice: x: 2, y: 2, z: 4, core: 2. Of those that a mesh axis runs over, the one named last changes fastest.
Arguments:
- context: bfloat16 [8192, 1024], P(('groups', 'ctx', 'head')), parts along dimension 0, may hold values from -6 to 6
- w_kv: bfloat16 [1024, 2048], replicated, may hold values from -0.1875 to 0.1875
- queries: bfloat16 [32, 64, 2048], P(('groups', 'head')), parts along dimension 0, may hold values from -400 to 400
- gain: float32 [1024], replicated, may hold values from 0.25 to 1.75
- w_out: bfloat16 [1024, 1024], P('head'), may hold values from -0.1875 to 0.1875
Outputs:
- latent_out: bfloat16 [4096, 1024], P(('groups', 'ctx', 'head')), parts along dimension 0
There are 2 independent parts, one for each index of `groups`. A program takes and returns all parts, laid end to end along the dimension named above; an argument that names none is the same for every part. Nothing has to cross between parts.
All inputs are finite; a program needn't handle non-finite values.
Results may differ from a plain program's by a relative error of at most 0.01575.
Values may be sent and summed in bfloat16 or wider, within the bound.
A program may use at most 64 MiB of HBM per device.

v0:
```python
import math

import jax
import jax.numpy as jnp
from jax import lax
from jax.sharding import PartitionSpec as P

epsilon = 1e-06


def body(context, w_kv, queries, gain, w_out):
    heads_local, head_size, latents = queries.shape
    model_width = w_kv.shape[0]
    total_heads = w_kv.shape[1] // (2 * head_size)
    head_count = lax.axis_size("head")
    ctx_count = lax.axis_size("ctx")
    head_scale = 1.0 / math.sqrt(head_size)
    projected = jnp.dot(context, w_kv, preferred_element_type=jnp.float32).astype(jnp.bfloat16)
    projected = projected.reshape(context.shape[0], total_heads, 2 * head_size)
    regrouped = lax.all_to_all(projected, "head", split_axis=1, concat_axis=0, tiled=True)
    key_rows = regrouped[:, :, :head_size]
    value_rows = regrouped[:, :, head_size:]
    block_size = min(512, latents)
    block_count = latents // block_size
    query_blocks = queries.reshape(heads_local, head_size, block_count, block_size)

    def attend(position):
        query_block = lax.dynamic_index_in_dim(query_blocks, position, 2, keepdims=False)
        scores = (
            jnp.einsum("hdq,khd->hqk", query_block, key_rows, preferred_element_type=jnp.float32)
            * head_scale
        )
        highest = jnp.max(scores, axis=2)
        weights = jnp.exp(scores - highest[:, :, None])
        row_total = jnp.sum(weights, axis=2)
        summed = jnp.einsum(
            "hqk,khd->hqd",
            weights.astype(jnp.bfloat16),
            value_rows,
            preferred_element_type=jnp.float32,
        )
        return (highest, row_total, summed)

    maxima, totals, partials = lax.map(attend, jnp.arange(block_count))
    maxima = maxima.transpose(1, 0, 2).reshape(heads_local, latents)
    totals = totals.transpose(1, 0, 2).reshape(heads_local, latents)
    partials = partials.transpose(1, 0, 2, 3).reshape(heads_local, latents * head_size // 128, 128)
    ctx_rows = latents // ctx_count
    overall = lax.pmax(maxima, "ctx")
    factor = jnp.exp(maxima - overall)
    spread = partials.reshape(heads_local, latents, head_size) * factor[:, :, None]
    scaled = spread.reshape(heads_local, latents * head_size // 128, 128)
    sums_own, total_own = (
        lax.psum_scatter(
            scaled.astype(jnp.bfloat16), "ctx", scatter_dimension=1, tiled=True
        ).astype(jnp.float32),
        lax.psum_scatter(
            (totals * factor).astype(jnp.bfloat16), "ctx", scatter_dimension=1, tiled=True
        ).astype(jnp.float32),
    )
    sums_own = sums_own.reshape(heads_local, ctx_rows, head_size)
    attended = sums_own / total_own[:, :, None]
    own_rows = ctx_rows // head_count
    packed = attended.reshape(heads_local, head_count, own_rows * head_size)
    gathered = lax.all_to_all(
        packed.astype(jnp.bfloat16), "head", split_axis=1, concat_axis=0, tiled=True
    ).astype(packed.dtype)
    joined = (
        gathered.reshape(total_heads, own_rows, head_size)
        .transpose(1, 0, 2)
        .reshape(own_rows, model_width)
    )
    mean_square = jnp.sum(joined * joined, axis=1, keepdims=True) / model_width
    normed = (joined * gain[None, :] * lax.rsqrt(mean_square + epsilon)).astype(jnp.bfloat16)
    result = jnp.dot(
        normed,
        lax.all_gather(w_out, "head", axis=0, tiled=True),
        preferred_element_type=jnp.float32,
    )
    return result.astype(jnp.bfloat16)


def solution(mesh):
    return jax.shard_map(
        body,
        mesh=mesh,
        in_specs=(
            P(("groups", "ctx", "head"), None),
            P(),
            P(("groups", "head"), None, None),
            P(),
            P("head", None),
        ),
        out_specs=P(("groups", "ctx", "head"), None),
        check_vma=False,
    )
```

profile of v0, /device:TPU:0, one launch (start us, length us, event | category | flops | bytes accessed | tf_op | source)
XLA Modules:
  0.0 184.9 jit_solution(581980694861545381)
XLA Ops:
  8.4 3.4 %fusion.15 = bf16[32,16,8,128]{3,2,1,0:T(8,128)(2,1)S(1)} fusion(bf16[256,1024]{1,0:T(8,128)(2,1)S(1)} %copy-done, bf16[1024,2048]{1,0:T(8,128)(2,1)} %param.8), kind=kOutput, calls=%fused_computation.16 | convolution fusion | flops 1074266112 | bytes 5767168 | tf_op jit(solution)/shard_map/dot_general | solution.py:18
  13.1 6.3 %all-to-all-start = ((bf16[256,16,128]{2,0,1:T(8,128)(2,1)}), bf16[256,16,128]{2,0,1:T(8,128)(2,1)S(1)}, u32[]{:S(2)}, u32[]{:S(2)}) async-start(bf16[256,16,128]{2,0,1:T(8,128)(2,1)} %bitcast.58), calls=%async_computation | async-start | bytes 2097152 | tf_op jit(solution)/shard_map/all_to_all | solution.py:20
  20.8 24.4 %all-to-all-done = bf16[256,16,128]{2,0,1:T(8,128)(2,1)S(1)} async-done(((bf16[256,16,128]{2,0,1:T(8,128)(2,1)}), bf16[256,16,128]{2,0,1:T(8,128)(2,1)S(1)}, u32[]{:S(2)}, u32[]{:S(2)}) %all-to-all-start) | async-done | bytes 1048608 | tf_op jit(solution)/shard_map/all_to_all | solution.py:20
  45.2 1.5 copy.13
  46.6 2.6 %all_to_all.23 = bf16[1024,4,128]{0,2,1:T(8,128)(2,1)} reshape(bf16[4,256,4,128]{1,0,3,2:T(4,128)(2,1)} %copy.13) | data formatting | bytes 2097152 | tf_op jit(solution)/shard_map/all_to_all | solution.py:20
  50.5 32.3 %while.14 = (s32[]{:T(128)}, f32[4,4,512]{2,1,0:T(4,128)S(1)}, f32[4,4,512]{2,1,0:T(4,128)S(1)}, f32[4,4,512,64]{2,3,1,0:T(8,128)}, s32[4]{0:T(128)S(1)}, /*inde...) while((s32[]{:T(128)}, f32[4,4,512]{2,1,0:T(4,128)S(1)}, ...), condition=%wide.region_3.4_spmd, body=%wide.region_0.3_spmd.sunk | while | flops 553644032 | bytes 27067044 | solution.py:44
  54.2 2.6 %fusion.34 = f32[4,4,512,64]{2,3,1,0:T(8,128)} fusion(f32[4,4,512,64]{2,3,1,0:T(8,128)} %get-tuple-element.163, s32[]{:T(128)} %get-tuple-element.160, bf16[1024,4,64]{0,2,1:T(8,128)(2,1)S(1)} %get-tuple-element.178, f32[4,512,1024]{2,1,0:T(8,128)S(1)} %get-tuple-element.145, f32[4,512]{1,0:T(4,128)S(1)} %get-tuple-element.146), kind=kOutput, calls=%fused_computation.6.clone.1 | convolution fusion | flops 274726912 | bytes 9445888 | tf_op jit(solution)/shard_map/while/body/eval_jaxpr/hqk,khd->hqd/dot_general | solution.py:36
  56.7 1.8 fusion.33
  62.2 2.6 %fusion.34 = f32[4,4,512,64]{2,3,1,0:T(8,128)} fusion(f32[4,4,512,64]{2,3,1,0:T(8,128)} %get-tuple-element.163, s32[]{:T(128)} %get-tuple-element.160, bf16[1024,4,64]{0,2,1:T(8,128)(2,1)S(1)} %get-tuple-element.178, f32[4,512,1024]{2,1,0:T(8,128)S(1)} %get-tuple-element.145, f32[4,512]{1,0:T(4,128)S(1)} %get-tuple-element.146), kind=kOutput, calls=%fused_computation.6.clone.1 | convolution fusion | flops 274726912 | bytes 9445888 | tf_op jit(solution)/shard_map/while/body/eval_jaxpr/hqk,khd->hqd/dot_general | solution.py:36
  64.8 1.8 fusion.33
  70.3 2.6 %fusion.34 = f32[4,4,512,64]{2,3,1,0:T(8,128)} fusion(f32[4,4,512,64]{2,3,1,0:T(8,128)} %get-tuple-element.163, s32[]{:T(128)} %get-tuple-element.160, bf16[1024,4,64]{0,2,1:T(8,128)(2,1)S(1)} %get-tuple-element.178, f32[4,512,1024]{2,1,0:T(8,128)S(1)} %get-tuple-element.145, f32[4,512]{1,0:T(4,128)S(1)} %get-tuple-element.146), kind=kOutput, calls=%fused_computation.6.clone.1 | convolution fusion | flops 274726912 | bytes 9445888 | tf_op jit(solution)/shard_map/while/body/eval_jaxpr/hqk,khd->hqd/dot_general | solution.py:36
  72.9 1.8 fusion.33
  78.4 2.6 %fusion.34 = f32[4,4,512,64]{2,3,1,0:T(8,128)} fusion(f32[4,4,512,64]{2,3,1,0:T(8,128)} %get-tuple-element.163, s32[]{:T(128)} %get-tuple-element.160, bf16[1024,4,64]{0,2,1:T(8,128)(2,1)S(1)} %get-tuple-element.178, f32[4,512,1024]{2,1,0:T(8,128)S(1)} %get-tuple-element.145, f32[4,512]{1,0:T(4,128)S(1)} %get-tuple-element.146), kind=kOutput, calls=%fused_computation.6.clone.1 | convolution fusion | flops 274726912 | bytes 9445888 | tf_op jit(solution)/shard_map/while/body/eval_jaxpr/hqk,khd->hqd/dot_general | solution.py:36
  81.0 1.8 fusion.33
  82.8 10.3 %pmax.7 = f32[4,2048]{1,0:T(4,128)S(1)} all-reduce(f32[4,2048]{1,0:T(4,128)S(1)} %bitcast.79), channel_id=1, replica_groups=mesh['groups'=2,'ctx'=4,'head'=4] {'ctx'}, use_global_device_ids=true, to_apply=%region_4.5 | all-reduce | flops 8192 | bytes 65536 | tf_op jit(solution)/shard_map/pmax | solution.py:49
  93.2 2.6 %mul.37 = f32[4,2048,64]{2,1,0:T(8,128)} broadcast(f32[4,2048]{1,0:T(4,128)S(1)} %get-tuple-element.85), dimensions={0,1} | broadcast | bytes 2129920 | tf_op jit(solution)/shard_map/mul | solution.py:51
  95.7 4.6 %mul.38 = f32[4,1024,128]{2,1,0:T(8,128)} reshape(f32[4,2048,64]{2,1,0:T(8,128)} %mul.37) | data formatting | bytes 4194304 | tf_op jit(solution)/shard_map/mul | solution.py:51
  100.4 3.8 %copy.15 = f32[4,4,512,64]{3,2,1,0:T(8,128)} copy(f32[4,4,512,64]{2,3,0,1:T(8,128)} %bitcast.75) | data formatting | bytes 4194304 | tf_op jit(solution)/shard_map/transpose | solution.py:47
  104.2 4.6 %reshape_reshape.3 = f32[4,1024,128]{2,1,0:T(8,128)} reshape(f32[4,4,512,64]{3,2,1,0:T(8,128)} %copy.15) | data formatting | bytes 4194304 | tf_op jit(solution)/shard_map/reshape;reshape | solution.py:51
  109.9 3.4 %multiply_convert_fusion = bf16[4,1024,128]{2,1,0:T(8,128)(2,1)} fusion(f32[4,1024,128]{2,1,0:T(8,128)} %reshape_reshape.3, f32[4,1024,128]{2,1,0:T(8,128)} %mul.38), kind=kLoop, calls=%fused_computation.15 | loop fusion | flops 1048576 | bytes 5242880 | tf_op jit(solution)/shard_map/convert_element_type | solution.py:55
  113.9 17.0 %reduce-scatter.7.cloned.1.call-done = bf16[512,4]{1,0:T(8,128)(2,1)} async-done(((bf16[2048,4]{1,0:T(8,128)(2,1)}), bf16[512,4]{1,0:T(8,128)(2,1)}) %reduce-scatter.7.cloned.1.call-update) | async-done | bytes 4112
  132.7 25.9 %reduce-scatter.5.cloned.1.call-done = bf16[4,256,128]{2,1,0:T(8,128)(2,1)} async-done(((bf16[4,1024,128]{2,1,0:T(8,128)(2,1)}), bf16[4,256,128]{2,1,0:T(8,128)(2,1)}) %reduce-scatter.5.cloned.1.call-update) | async-done | bytes 262160 | tf_op jit(solution)/shard_map/reduce_scatter | solution.py:54
  160.1 13.2 %all_to_all.27 = bf16[4,4,8192]{2,0,1:T(4,128)(2,1)S(1)} all-to-all(bf16[4,4,8192]{2,0,1:T(4,128)(2,1)S(1)} %copy.16), channel_id=1, replica_groups=mesh['groups'=2,'ctx'=4,'head'=4] {'head'}, dimensions={1} | all-to-all | bytes 524288 | tf_op jit(solution)/shard_map/all_to_all | solution.py:65
  174.7 2.8 %convolution_convert_fusion.1 = bf16[128,1024]{1,0:T(8,128)(2,1)} fusion(bf16[128,1024]{0,1:T(8,128)(2,1)S(1)} %fusion.17, bf16[1024,1024]{1,0:T(8,128)(2,1)} %all-gather.2.cloned.1.call-done), kind=kOutput, calls=%fused_computation.17 | convolution fusion | flops 268566528 | bytes 2621440 | tf_op jit(solution)/shard_map/dot_general | solution.py:75
  (44 shorter events, 19.2 us)
Async XLA Ops:
  7.4 1.0 copy-start
  13.1 32.0 %all-to-all-start = ((bf16[256,16,128]{2,0,1:T(8,128)(2,1)}), bf16[256,16,128]{2,0,1:T(8,128)(2,1)S(1)}, u32[]{:S(2)}, u32[]{:S(2)}) async-start(bf16[256,16,128]{2,0,1:T(8,128)(2,1)} %bitcast.58), calls=%async_computation | async-start | bytes 2097152 | tf_op jit(solution)/shard_map/all_to_all | solution.py:20
  19.4 111.5 %reduce-scatter.7.cloned.1.call-start = ((), (), s32[]{:S(2)}) async-start(), calls=%async_computation.6 | async-start | bytes 655360
  109.9 48.7 %reduce-scatter.5.cloned.1.call-start = ((), (), s32[]{:S(2)}) async-start(), calls=%async_computation.4 | async-start | bytes 1310720 | tf_op jit(solution)/shard_map/reduce_scatter | solution.py:54
  113.4 61.3 %all-gather.2.cloned.1.call-start = ((), (), s32[]{:S(2)}) async-start(), calls=%async_computation.5 | async-start | bytes 2621440 | tf_op jit(solution)/shard_map/all_gather | solution.py:77
  132.7 41.7 %copy-start.1 = (f32[1024]{0:T(1024)S(1)}, f32[1024]{0:T(1024)}, u32[]{:S(2)}) copy-start(f32[1024]{0:T(1024)} %param.10) | copy-start | bytes 12292
Sparse Core Ops, SparseCore 0:
  110.0 20.8 reduce-scatter.6
  133.6 24.9 reduce-scatter.4
Sparse Core Ops, SparseCore 1:
  115.4 44.7 all-gather.1
where the time goes:
time: 186 us; the launch traced here: 185 us
  waiting for transfers between devices  67.8 us (36%)
  local copies, waits for them, and re-layouts  32 us (17%)
  blocking collectives  23.5 us (13%)
  matrix products  22.1 us (12%)
  between operations  15 us (8%)
  other arithmetic  11.3 us (6%)
  loops' own time  6.81 us (4%)
  starting transfers between devices  6.41 us (3%)
    reduce_scatter x1, waiting for transfers between devices, body(): lax.psum_scatter(scaled.astype(jnp.bfloat16), 'ctx', scatter_dimension=1,...  25.9 us
    all_to_all x1, waiting for transfers between devices, body(): lax.all_to_all(projected, 'head', split_axis=1, concat_axis=0, tiled=True)  24.4 us
    unnamed x4, waiting for transfers between devices  17.5 us
    all_to_all x1, blocking collectives, body(): lax.all_to_all(packed.astype(jnp.bfloat16), 'head', split_axis=1, concat_...  13.2 us
    dot_general x4, matrix products, attend(): jnp.einsum('hqk,khd->hqd', weights.astype(jnp.bfloat16), value_rows, pref...  10.3 us
    pmax x1, blocking collectives, body(): overall = lax.pmax(maxima, 'ctx')  10.3 us
    mul x2, local copies, waits for them, and re-layouts, body(): partials.reshape(heads_local, latents, head_size) * factor[:, :, None]  7.21 us
    reduce_sum x4, other arithmetic, attend(): row_total = jnp.sum(weights, axis=2)  7.21 us
  transfers between devices with their start and end apart: 4, of which 3 were waited for; matrix products, arithmetic and copies ran while one was open for 5% of the time, Pallas kernels for 0%

commit v1 on v0

v1 whole, which is shorter than its diff:
```python
import functools
import math

import jax
import jax.numpy as jnp
from jax import lax
from jax.experimental import pallas as pl
from jax.experimental.pallas import tpu as pltpu
from jax.sharding import PartitionSpec as P

epsilon = 1e-06
MESH = pl.DeviceIdType.MESH


def attention_kernel(
    n_head, n_ctx, q_tile,
    context_ref, w_kv_ref, queries_ref, gain_ref,
    normed_ref,
    kv_send, kv_all, acc, high, total, head_out, head_in, *rest,
):
    n_stage = n_ctx.bit_length() - 1
    sum_send, rest = rest[:n_stage], rest[n_stage:]
    sum_recv, rest = rest[:n_stage], rest[n_stage:]
    stat_send, rest = rest[:n_stage], rest[n_stage:]
    stat_recv, rest = rest[:n_stage], rest[n_stage:]
    kv_ssem, kv_rsem, sum_ssem, sum_rsem, stat_ssem, stat_rsem, out_ssem, out_rsem = rest

    heads_local, head_size, latents = queries_ref.shape
    width = 2 * head_size
    group_width = heads_local * width
    ctx_rows = latents // n_ctx
    own_rows = ctx_rows // n_head
    scale = math.log2(math.e) / math.sqrt(head_size)
    my_head = lax.axis_index("head")
    my_ctx = lax.axis_index("ctx")

    barrier = pltpu.get_barrier_semaphore()
    for mask in range(1, n_head):
        pl.semaphore_signal(
            barrier, inc=1, device_id={"head": my_head ^ mask}, device_id_type=MESH
        )
    for stage in range(n_stage):
        pl.semaphore_signal(
            barrier, inc=1, device_id={"ctx": my_ctx ^ (1 << stage)}, device_id_type=MESH
        )

    def project(target):
        columns = pl.ds(pl.multiple_of(target * group_width, group_width), group_width)
        return jnp.dot(
            context_ref[...], w_kv_ref[:, columns], preferred_element_type=jnp.float32
        ).astype(jnp.bfloat16)

    kv_copies = {}
    for mask in range(n_head - 1, 0, -1):
        kv_send[mask - 1] = project(my_head ^ mask)
        if mask == n_head - 1:
            pl.semaphore_wait(barrier, n_head - 1 + n_stage)
        kv_copies[mask] = pltpu.make_async_remote_copy(
            src_ref=kv_send.at[mask - 1],
            dst_ref=kv_all.at[mask],
            send_sem=kv_ssem.at[mask - 1],
            recv_sem=kv_rsem.at[mask - 1],
            device_id={"head": my_head ^ mask},
            device_id_type=MESH,
        )
        kv_copies[mask].start()
    kv_all[0] = project(my_head)

    def attend(slot, head, first):
        columns = pl.ds(pl.multiple_of(head * width, width), width)
        block = kv_all[slot, :, columns]
        key = block[:, :head_size]
        value = block.T[head_size:, :]
        for tile in range(latents // q_tile):
            span = slice(tile * q_tile, (tile + 1) * q_tile)
            scores = (
                jnp.dot(key, queries_ref[head, :, span], preferred_element_type=jnp.float32)
                * scale
            )
            highest = jnp.max(scores, axis=0, keepdims=True)
            if not first:
                before = high[head, :, span]
                highest = jnp.maximum(highest, before)
                factor = jnp.exp2(before - highest)
            weights = jnp.exp2(scores - highest)
            row_total = jnp.sum(weights, axis=0, keepdims=True)
            summed = jnp.dot(
                value, weights.astype(jnp.bfloat16), preferred_element_type=jnp.float32
            )
            if not first:
                row_total += total[head, :, span] * factor
                summed += acc[head, :, span] * factor
            high[head, :, span] = highest
            total[head, :, span] = row_total
            acc[head, :, span] = summed

    order = [0] + ([1] if n_head > 1 else []) + list(range(n_head - 1, 1, -1))
    for slot in order[:-1]:
        if slot:
            kv_copies[slot].wait_recv()

        def one_head(head, carry, slot=slot):
            attend(slot, head, slot == 0)
            return carry

        lax.fori_loop(0, heads_local, one_head, 0)
    last = order[-1]
    if last:
        kv_copies[last].wait_recv()

    copies = []
    pending = {}
    held = {}

    def chunk(head, stage, index):
        if stage == 0:
            span = pl.ds(pl.multiple_of(index * ctx_rows, ctx_rows), ctx_rows)
            return acc[head, :, span], high[head, :, span], total[head, :, span]
        source = pl.ds(pl.multiple_of(index * ctx_rows, ctx_rows), ctx_rows)
        return acc[head, :, source], high[head, :, source], total[head, :, source]

    def send_stage(head, stage):
        bit = (my_ctx >> stage) & 1
        for t in range(n_ctx >> (stage + 1)):
            value, top, weight = chunk(head, stage, 2 * t + 1 - bit)
            span = slice(t * ctx_rows, (t + 1) * ctx_rows)
            sum_send[stage][head, :, span] = value.astype(jnp.bfloat16)
            stat_send[stage][head, 0:1, span] = top
            stat_send[stage][head, 1:2, span] = weight
        pair = []
        for source, target, ssem, rsem in (
            (sum_send, sum_recv, sum_ssem, sum_rsem),
            (stat_send, stat_recv, stat_ssem, stat_rsem),
        ):
            copy = pltpu.make_async_remote_copy(
                src_ref=source[stage].at[head],
                dst_ref=target[stage].at[head],
                send_sem=ssem.at[stage, head],
                recv_sem=rsem.at[stage, head],
                device_id={"ctx": my_ctx ^ (1 << stage)},
                device_id_type=MESH,
            )
            copy.start()
            pair.append(copy)
        copies.extend(pair)
        pending[head, stage] = pair

    def merge_stage(head, stage):
        for copy in pending[head, stage]:
            copy.wait_recv()
        bit = (my_ctx >> stage) & 1
        merged = []
        for t in range(n_ctx >> (stage + 1)):
            value, top, weight = chunk(head, stage, 2 * t + bit)
            span = slice(t * ctx_rows, (t + 1) * ctx_rows)
            other = sum_recv[stage][head, :, span].astype(jnp.float32)
            other_top = stat_recv[stage][head, 0:1, span]
            other_weight = stat_recv[stage][head, 1:2, span]
            highest = jnp.maximum(top, other_top)
            mine = jnp.exp2(top - highest)
            theirs = jnp.exp2(other_top - highest)
            merged.append((
                value * mine + other * theirs,
                highest,
                weight * mine + other_weight * theirs,
            ))
            if stage + 1 < n_stage:
                acc[head, :, span], high[head, :, span], total[head, :, span] = merged[-1]
        return merged[0]

    def send_out(head, value, weight):
        attended = (value / weight).astype(jnp.bfloat16)
        for piece in range(n_head):
            head_out[piece, head] = attended[:, piece * own_rows:(piece + 1) * own_rows]
        for mask in range(1, n_head):
            copy = pltpu.make_async_remote_copy(
                src_ref=head_out.at[my_head ^ mask, head],
                dst_ref=head_in.at[my_head, head],
                send_sem=out_ssem.at[mask - 1, head],
                recv_sem=out_rsem.at[mask - 1, head],
                device_id={"head": my_head ^ mask},
                device_id_type=MESH,
            )
            copy.start()
            copies.append(copy)
            pending["out", head, mask] = copy
        head_in[my_head, head] = head_out[my_head, head]

    def advance(head, stage):
        merged = merge_stage(head, stage)
        if stage + 1 < n_stage:
            send_stage(head, stage + 1)
        else:
            send_out(head, merged[0], merged[2])

    for step in range(heads_local + n_stage):
        if step < heads_local:
            attend(last, step, last == 0)
            send_stage(step, 0)
        for stage in range(n_stage):
            head = step - 1 - stage
            if 0 <= head < heads_local:
                advance(head, stage)

    for head in range(heads_local):
        for mask in range(1, n_head):
            pending["out", head, mask].wait_recv()
    joined = head_in[...].astype(jnp.float32).reshape(
        n_head * heads_local * head_size, own_rows
    )
    mean_square = jnp.sum(joined * joined, axis=0, keepdims=True) / joined.shape[0]
    normed_ref[...] = (
        joined * gain_ref[...] * lax.rsqrt(mean_square + epsilon)
    ).astype(jnp.bfloat16)

    for mask in range(1, n_head):
        kv_copies[mask].wait_send()
    for copy in copies:
        copy.wait_send()


def body(context, w_kv, queries, gain, w_out):
    heads_local, head_size, latents = queries.shape
    model_width = w_kv.shape[0]
    n_head = lax.axis_size("head")
    n_ctx = lax.axis_size("ctx")
    n_stage = n_ctx.bit_length() - 1
    rows = context.shape[0]
    ctx_rows = latents // n_ctx
    own_rows = ctx_rows // n_head
    group_width = heads_local * 2 * head_size
    w_full = lax.all_gather(w_out, "head", axis=0, tiled=True)

    def stage_buffers(depth, kind):
        return [
            pltpu.VMEM((heads_local, depth, (n_ctx >> (s + 1)) * ctx_rows), kind)
            for s in range(n_stage)
        ]

    dma = pltpu.SemaphoreType.DMA
    vmem = pl.BlockSpec(memory_space=pltpu.VMEM)
    normed = pl.pallas_call(
        functools.partial(attention_kernel, n_head, n_ctx, min(512, latents)),
        out_shape=jax.ShapeDtypeStruct((model_width, own_rows), jnp.bfloat16),
        in_specs=[vmem] * 4,
        out_specs=vmem,
        scratch_shapes=[
            pltpu.VMEM((n_head - 1, rows, group_width), jnp.bfloat16),
            pltpu.VMEM((n_head, rows, group_width), jnp.bfloat16),
            pltpu.VMEM((heads_local, head_size, latents), jnp.float32),
            pltpu.VMEM((heads_local, 1, latents), jnp.float32),
            pltpu.VMEM((heads_local, 1, latents), jnp.float32),
            pltpu.VMEM((n_head, heads_local, head_size, own_rows), jnp.bfloat16),
            pltpu.VMEM((n_head, heads_local, head_size, own_rows), jnp.bfloat16),
            *stage_buffers(head_size, jnp.bfloat16),
            *stage_buffers(head_size, jnp.bfloat16),
            *stage_buffers(2, jnp.float32),
            *stage_buffers(2, jnp.float32),
            dma((n_head - 1,)),
            dma((n_head - 1,)),
            dma((n_stage, heads_local)),
            dma((n_stage, heads_local)),
            dma((n_stage, heads_local)),
            dma((n_stage, heads_local)),
            dma((n_head - 1, heads_local)),
            dma((n_head - 1, heads_local)),
        ],
        compiler_params=pltpu.CompilerParams(
            collective_id=0, has_side_effects=True, vmem_limit_bytes=48 * 1024 * 1024
        ),
        cost_estimate=pl.CostEstimate(
            flops=4 * heads_local * latents * rows * n_head * head_size
            + 4 * rows * model_width * model_width,
            bytes_accessed=2 * w_kv.size + 2 * context.size + 2 * queries.size,
            transcendentals=heads_local * latents * rows * n_head,
        ),
    )(context, w_kv, queries, gain.reshape(model_width, 1))
    result = lax.dot_general(
        normed, w_full, (((0,), (0,)), ((), ())), preferred_element_type=jnp.float32
    )
    return result.astype(jnp.bfloat16)


def solution(mesh):
    return jax.shard_map(
        body,
        mesh=mesh,
        in_specs=(
            P(("groups", "ctx", "head"), None),
            P(),
            P(("groups", "head"), None, None),
            P(),
            P("head", None),
        ),
        out_specs=P(("groups", "ctx", "head"), None),
        check_vma=False,
    )
```

time: 186 us -> 95.8 us (0.52)
  Pallas kernels: 0 us -> 75.5 us
  waiting for transfers between devices: 67.8 us -> 0.73 us
  local copies, waits for them, and re-layouts: 32 us -> 3.17 us
  blocking collectives: 23.5 us -> 0 us
  matrix products: 22.1 us -> 2.77 us
  other arithmetic: 11.3 us -> 0 us
  loops' own time: 6.81 us -> 0 us
  starting transfers between devices: 6.41 us -> 0.01 us
    pallas_call x0 -> x1, Pallas kernels: none -> 75.5 us  [body(): pl.pallas_call(functools.partial(attention_kernel, n_head, n_ctx, min(512...]
    reduce_scatter x1 -> x0, waiting for transfers between devices: 25.9 us -> none  [body(): lax.psum_scatter(scaled.astype(jnp.bfloat16), 'ctx', scatter_dimension=1,...]
    all_to_all x1 -> x0, waiting for transfers between devices: 24.4 us -> none  [body(): lax.all_to_all(projected, 'head', split_axis=1, concat_axis=0, tiled=True)]
    dot_general x10 -> x1, matrix products: 22.1 us -> 2.77 us  [body(): lax.dot_general(normed, w_full, (((0,), (0,)), ((), ())), preferred_eleme...]
    unnamed x4 -> x1, waiting for transfers between devices: 17.5 us -> 0.71 us
    all_to_all x1 -> x0, blocking collectives: 13.2 us -> none  [body(): lax.all_to_all(packed.astype(jnp.bfloat16), 'head', split_axis=1, concat_...]
    pmax x1 -> x0, blocking collectives: 10.3 us -> none  [body(): overall = lax.pmax(maxima, 'ctx')]
    reduce_sum x5 -> x0, other arithmetic: 7.41 us -> none  [the longest x4 7.21 us: attend(): row_total = jnp.sum(weights, axis=2)]
  transfers between devices with their start and end apart: 4 -> 1, of which waited for: 3 -> 0; matrix products, arithmetic and copies ran while one was open for 5% -> 1% of each run, Pallas kernels for 0% -> 79%
where the time goes in v1:
time: 95.8 us; the launch traced here: 95.6 us
  Pallas kernels  75.5 us (79%)
  between operations  13.4 us (14%)
  local copies, waits for them, and re-layouts  3.17 us (3%)
  matrix products  2.77 us (3%)
    pallas_call x1, Pallas kernels, body(): pl.pallas_call(functools.partial(attention_kernel, n_head, n_ctx, min(512...  75.5 us
    dot_general x1, matrix products, body(): lax.dot_general(normed, w_full, (((0,), (0,)), ((), ())), preferred_eleme...  2.77 us
    unnamed x4, local copies, waits for them, and re-layouts  2.26 us
  transfers between devices with their start and end apart: 1, of which 0 were waited for; matrix products, arithmetic and copies ran while one was open for 1% of the time, Pallas kernels for 79%

profile of v1, /device:TPU:0, one launch (start us, length us, event | category | flops | bytes accessed | tf_op | source)
XLA Modules:
  0.0 95.6 jit_solution(10098733792150613981)
XLA Ops:
  6.5 0.0 all-gather.2.cloned.1.call-start
  6.5 0.7 all-gather.2.cloned.1.call-update
  7.3 0.9 copy.6.gain_ref
  8.2 0.0 copy-start
  8.2 1.2 %copy-done = bf16[4,64,2048]{2,1,0:T(8,128)(2,1)S(1)} copy-done((bf16[4,64,2048]{2,1,0:T(8,128)(2,1)S(1)}, bf16[4,64,2048]{2,1,0:T(8,128)(2,1)}, u32[]{:S(2)}) %copy-start) | copy-done | bytes 1048600
  9.4 0.0 copy-start.1
  9.4 1.0 %copy-done.1 = bf16[256,1024]{1,0:T(8,128)(2,1)S(1)} copy-done((bf16[256,1024]{1,0:T(8,128)(2,1)S(1)}, bf16[256,1024]{1,0:T(8,128)(2,1)}, u32[]{:S(2)}) %copy-start.1) | copy-done | bytes 524312
  10.4 75.5 %shard_map.55 = bf16[1024,128]{1,0:T(8,128)(2,1)S(1)} custom-call(bf16[256,1024]{1,0:T(8,128)(2,1)S(1)} %copy-done.1, bf16[1024,2048]{1,0:T(8,128)(2,1)} %w_kv_ref.1, bf16[4,64,2048]{2,1,0:T(8,128)(2,1)S(1)} %copy-done, f32[1024,1]{1,0:T(8,128)S(1)} %copy.6.gain_ref), custom_call_target="tpu_custom_call" | custom-call | flops 3221225472 | bytes 5767168 | tf_op jit(solution)/shard_map/pallas_call | solution.py:242
  85.9 0.0 all-gather.2.cloned.1.call-done
  85.9 2.8 %convolution_convert_fusion = bf16[128,1024]{1,0:T(8,128)(2,1)} fusion(bf16[1024,128]{1,0:T(8,128)(2,1)S(1)} %shard_map.55, bf16[1024,1024]{1,0:T(8,128)(2,1)} %all-gather.2.cloned.1.call-done), kind=kOutput, calls=%fused_computation | convolution fusion | flops 268566528 | bytes 2621440 | tf_op jit(solution)/shard_map/dot_general | solution.py:278
Async XLA Ops:
  6.5 79.4 %all-gather.2.cloned.1.call-start = ((), (), s32[]{:S(2)}) async-start(), calls=%async_computation | async-start | bytes 2621440 | tf_op jit(solution)/shard_map/all_gather | solution.py:232
  8.2 1.2 %copy-start = (bf16[4,64,2048]{2,1,0:T(8,128)(2,1)S(1)}, bf16[4,64,2048]{2,1,0:T(8,128)(2,1)}, u32[]{:S(2)}) copy-start(bf16[4,64,2048]{2,1,0:T(8,128)(2,1)} %queries_ref.1) | copy-start | bytes 3145732
  9.4 1.0 %copy-start.1 = (bf16[256,1024]{1,0:T(8,128)(2,1)S(1)}, bf16[256,1024]{1,0:T(8,128)(2,1)}, u32[]{:S(2)}) copy-start(bf16[256,1024]{1,0:T(8,128)(2,1)} %context_ref.1) | copy-start | bytes 1572868
Sparse Core Ops, SparseCore 0:
  8.9 69.5 all-gather.1

commit v2 on v1

--- a/solution.py
+++ b/solution.py
@@ -13,17 +13,18 @@
 
 
 def attention_kernel(
-    n_head, n_ctx, q_tile,
-    context_ref, w_kv_ref, queries_ref, gain_ref,
-    normed_ref,
-    kv_send, kv_all, acc, high, total, head_out, head_in, *rest,
+    n_head, n_ctx, n_part, q_tile,
+    context_ref, w_kv_ref, queries_ref, gain_ref, w_out_ref,
+    out_ref,
+    kv_send, kv_all, acc, high, total, head_out, head_in, w_all, *rest,
 ):
     n_stage = n_ctx.bit_length() - 1
     sum_send, rest = rest[:n_stage], rest[n_stage:]
     sum_recv, rest = rest[:n_stage], rest[n_stage:]
     stat_send, rest = rest[:n_stage], rest[n_stage:]
     stat_recv, rest = rest[:n_stage], rest[n_stage:]
-    kv_ssem, kv_rsem, sum_ssem, sum_rsem, stat_ssem, stat_rsem, out_ssem, out_rsem = rest
+    kv_ssem, kv_rsem, sum_ssem, sum_rsem, stat_ssem, stat_rsem, out_ssem, out_rsem = rest[:8]
+    wh_ssem, wh_rsem, wp_ssem, wp_rsem = rest[8:]
 
     heads_local, head_size, latents = queries_ref.shape
     width = 2 * head_size
@@ -33,6 +34,11 @@
     scale = math.log2(math.e) / math.sqrt(head_size)
     my_head = lax.axis_index("head")
     my_ctx = lax.axis_index("ctx")
+    my_group = lax.axis_index("groups")
+    ctx_parts = min(n_ctx, n_part)
+    group_bits = (n_part // ctx_parts).bit_length() - 1
+    my_part = (my_group & ((1 << group_bits) - 1)) * ctx_parts + (my_ctx & (ctx_parts - 1))
+    part_width = w_all.shape[3]
 
     barrier = pltpu.get_barrier_semaphore()
     for mask in range(1, n_head):
@@ -43,6 +49,12 @@
         pl.semaphore_signal(
             barrier, inc=1, device_id={"ctx": my_ctx ^ (1 << stage)}, device_id_type=MESH
         )
+    for level in range(group_bits):
+        pl.semaphore_signal(
+            barrier, inc=1, device_id={"groups": my_group ^ (1 << level)}, device_id_type=MESH
+        )
+    part_span = pl.ds(pl.multiple_of(my_part * part_width, part_width), part_width)
+    w_all[0, my_head] = w_out_ref[:, part_span]
 
     def project(target):
         columns = pl.ds(pl.multiple_of(target * group_width, group_width), group_width)
@@ -50,25 +62,109 @@
             context_ref[...], w_kv_ref[:, columns], preferred_element_type=jnp.float32
         ).astype(jnp.bfloat16)
 
+    weight_copies = []
+    w_pending = {}
+
+    def send_w(key, source, target, ssem, rsem, where):
+        copy = pltpu.make_async_remote_copy(
+            src_ref=source,
+            dst_ref=target,
+            send_sem=ssem,
+            recv_sem=rsem,
+            device_id=where,
+            device_id_type=MESH,
+        )
+        copy.start()
+        weight_copies.append(copy)
+        w_pending.setdefault(key, []).append(copy)
+
+    def receive_w(key):
+        for copy in w_pending[key]:
+            copy.wait_recv()
+
+    head_levels = list(reversed(range(n_head.bit_length() - 1)))
+    part_levels = list(reversed(range(n_part.bit_length() - 1)))
+    w_masks = {"head": [0], "part": [0]}
+
+    def w_head(level):
+        bit = 1 << level
+        for mask in w_masks["head"]:
+            index = (mask | bit) - 1
+            block = w_all.at[0, my_head ^ mask]
+            send_w(
+                ("head", level), block, block,
+                wh_ssem.at[index], wh_rsem.at[index], {"head": my_head ^ bit},
+            )
+        w_masks["head"] += [mask | bit for mask in w_masks["head"]]
+
+    def w_part(level):
+        bit = 1 << level
+        if bit >= ctx_parts:
+            where = {"groups": my_group ^ (bit // ctx_parts)}
+        else:
+            where = {"ctx": my_ctx ^ bit}
+        for mask in w_masks["part"]:
+            index = (mask | bit) - 1
+            send_w(
+                ("part", level), w_all.at[mask], w_all.at[mask | bit],
+                wp_ssem.at[index], wp_rsem.at[index], where,
+            )
+        w_masks["part"] += [mask | bit for mask in w_masks["part"]]
+
+    w_steps = [("head", level) for level in head_levels]
+    w_steps += [("part", level) for level in part_levels]
+    w_done = [0]
+
+    def advance_w():
+        index = w_done[0]
+        if index > len(w_steps):
+            return
+        if index:
+            receive_w(w_steps[index - 1])
+        if index < len(w_steps):
+            kind, level = w_steps[index]
+            (w_head if kind == "head" else w_part)(level)
+        w_done[0] = index + 1
+
+    near = [1] if n_head > 1 else []
+    far = list(range(n_head - 1, 1, -1))
     kv_copies = {}
-    for mask in range(n_head - 1, 0, -1):
-        kv_send[mask - 1] = project(my_head ^ mask)
-        if mask == n_head - 1:
-            pl.semaphore_wait(barrier, n_head - 1 + n_stage)
-        kv_copies[mask] = pltpu.make_async_remote_copy(
-            src_ref=kv_send.at[mask - 1],
-            dst_ref=kv_all.at[mask],
-            send_sem=kv_ssem.at[mask - 1],
-            recv_sem=kv_rsem.at[mask - 1],
+
+    def send_kv(mask, head):
+        kv_copies[mask, head] = pltpu.make_async_remote_copy(
+            src_ref=kv_send.at[mask - 1, head],
+            dst_ref=kv_all.at[mask, head],
+            send_sem=kv_ssem.at[mask - 1, head],
+            recv_sem=kv_rsem.at[mask - 1, head],
             device_id={"head": my_head ^ mask},
             device_id_type=MESH,
         )
-        kv_copies[mask].start()
-    kv_all[0] = project(my_head)
+        kv_copies[mask, head].start()
+
+    def project_into(mask, target):
+        projected = project(my_head ^ mask)
+        for head in range(heads_local):
+            target[mask - 1 if mask else 0, head] = projected[:, head * width:(head + 1) * width]
+
+    for mask in far + near:
+        project_into(mask, kv_send)
+        if mask == (far + near)[0]:
+            pl.semaphore_wait(barrier, n_head - 1 + n_stage + group_bits)
+            advance_w()
+        if len(far) > 1 and mask == far[0]:
+            send_kv(mask, 0)
+        elif far and mask == far[-1]:
+            for head in range(heads_local):
+                for other in far:
+                    if (other, head) not in kv_copies:
+                        send_kv(other, head)
+        elif mask == 1:
+            for head in range(heads_local):
+                send_kv(1, head)
+    project_into(0, kv_all)
 
     def attend(slot, head, first):
-        columns = pl.ds(pl.multiple_of(head * width, width), width)
-        block = kv_all[slot, :, columns]
+        block = kv_all[slot, head]
         key = block[:, :head_size]
         value = block.T[head_size:, :]
         for tile in range(latents // q_tile):
@@ -94,19 +190,17 @@
             total[head, :, span] = row_total
             acc[head, :, span] = summed
 
-    order = [0] + ([1] if n_head > 1 else []) + list(range(n_head - 1, 1, -1))
-    for slot in order[:-1]:
+    for slot in [0] + near:
         if slot:
-            kv_copies[slot].wait_recv()
+            advance_w()
+            for head in range(heads_local):
+                kv_copies[slot, head].wait_recv()
 
         def one_head(head, carry, slot=slot):
             attend(slot, head, slot == 0)
             return carry
 
         lax.fori_loop(0, heads_local, one_head, 0)
-    last = order[-1]
-    if last:
-        kv_copies[last].wait_recv()
 
     copies = []
     pending = {}
@@ -195,13 +289,18 @@
 
     for step in range(heads_local + n_stage):
         if step < heads_local:
-            attend(last, step, last == 0)
+            advance_w()
+            for mask in far:
+                kv_copies[mask, step].wait_recv()
+                attend(mask, step, False)
             send_stage(step, 0)
         for stage in range(n_stage):
             head = step - 1 - stage
             if 0 <= head < heads_local:
                 advance(head, stage)
 
+    while w_done[0] <= len(w_steps):
+        advance_w()
     for head in range(heads_local):
         for mask in range(1, n_head):
             pending["out", head, mask].wait_recv()
@@ -209,13 +308,16 @@
         n_head * heads_local * head_size, own_rows
     )
     mean_square = jnp.sum(joined * joined, axis=0, keepdims=True) / joined.shape[0]
-    normed_ref[...] = (
-        joined * gain_ref[...] * lax.rsqrt(mean_square + epsilon)
-    ).astype(jnp.bfloat16)
-
-    for mask in range(1, n_head):
-        kv_copies[mask].wait_send()
-    for copy in copies:
+    normed = (joined * gain_ref[...] * lax.rsqrt(mean_square + epsilon)).astype(jnp.bfloat16)
+    rows = normed.T
+    for mask in range(n_part):
+        weights = w_all[mask].reshape(joined.shape[0], part_width)
+        target = pl.ds(pl.multiple_of((my_part ^ mask) * part_width, part_width), part_width)
+        out_ref[:, target] = jnp.dot(
+            rows, weights, preferred_element_type=jnp.float32
+        ).astype(jnp.bfloat16)
+
+    for copy in list(kv_copies.values()) + weight_copies + copies:
         copy.wait_send()
 
 
@@ -228,8 +330,7 @@
     rows = context.shape[0]
     ctx_rows = latents // n_ctx
     own_rows = ctx_rows // n_head
-    group_width = heads_local * 2 * head_size
-    w_full = lax.all_gather(w_out, "head", axis=0, tiled=True)
+    n_part = min(lax.axis_size("groups") * n_ctx, model_width // 128)
 
     def stage_buffers(depth, kind):
         return [
@@ -239,31 +340,38 @@
 
     dma = pltpu.SemaphoreType.DMA
     vmem = pl.BlockSpec(memory_space=pltpu.VMEM)
-    normed = pl.pallas_call(
-        functools.partial(attention_kernel, n_head, n_ctx, min(512, latents)),
-        out_shape=jax.ShapeDtypeStruct((model_width, own_rows), jnp.bfloat16),
-        in_specs=[vmem] * 4,
+    return pl.pallas_call(
+        functools.partial(attention_kernel, n_head, n_ctx, n_part, min(1024, latents)),
+        out_shape=jax.ShapeDtypeStruct((own_rows, model_width), jnp.bfloat16),
+        in_specs=[vmem] * 5,
         out_specs=vmem,
         scratch_shapes=[
-            pltpu.VMEM((n_head - 1, rows, group_width), jnp.bfloat16),
-            pltpu.VMEM((n_head, rows, group_width), jnp.bfloat16),
+            pltpu.VMEM((n_head - 1, heads_local, rows, 2 * head_size), jnp.bfloat16),
+            pltpu.VMEM((n_head, heads_local, rows, 2 * head_size), jnp.bfloat16),
             pltpu.VMEM((heads_local, head_size, latents), jnp.float32),
             pltpu.VMEM((heads_local, 1, latents), jnp.float32),
             pltpu.VMEM((heads_local, 1, latents), jnp.float32),
             pltpu.VMEM((n_head, heads_local, head_size, own_rows), jnp.bfloat16),
             pltpu.VMEM((n_head, heads_local, head_size, own_rows), jnp.bfloat16),
+            pltpu.VMEM(
+                (n_part, n_head, w_out.shape[0], model_width // n_part), jnp.bfloat16
+            ),
             *stage_buffers(head_size, jnp.bfloat16),
             *stage_buffers(head_size, jnp.bfloat16),
             *stage_buffers(2, jnp.float32),
             *stage_buffers(2, jnp.float32),
-            dma((n_head - 1,)),
-            dma((n_head - 1,)),
+            dma((n_head - 1, heads_local)),
+            dma((n_head - 1, heads_local)),
             dma((n_stage, heads_local)),
             dma((n_stage, heads_local)),
             dma((n_stage, heads_local)),
             dma((n_stage, heads_local)),
             dma((n_head - 1, heads_local)),
             dma((n_head - 1, heads_local)),
+            dma((n_head - 1,)),
+            dma((n_head - 1,)),
+            dma((n_part - 1,)),
+            dma((n_part - 1,)),
         ],
         compiler_params=pltpu.CompilerParams(
             collective_id=0, has_side_effects=True, vmem_limit_bytes=48 * 1024 * 1024
@@ -274,11 +382,7 @@
             bytes_accessed=2 * w_kv.size + 2 * context.size + 2 * queries.size,
             transcendentals=heads_local * latents * rows * n_head,
         ),
-    )(context, w_kv, queries, gain.reshape(model_width, 1))
-    result = lax.dot_general(
-        normed, w_full, (((0,), (0,)), ((), ())), preferred_element_type=jnp.float32
-    )
-    return result.astype(jnp.bfloat16)
+    )(context, w_kv, queries, gain.reshape(model_width, 1), w_out)
 
 
 def solution(mesh):

time: 95.8 us -> 70.3 us (0.73)
  between operations: 13.4 us -> 0.03 us
  Pallas kernels: 75.5 us -> 65 us
  matrix products: 2.77 us -> 0 us
  local copies, waits for them, and re-layouts: 3.17 us -> 4.91 us
    pallas_call x1, Pallas kernels: 75.5 us -> 65 us  [body(): pl.pallas_call(functools.partial(attention_kernel, n_head, n_ctx, n_part,...]
    dot_general x1 -> x0, matrix products: 2.77 us -> none  [body(): lax.dot_general(normed, w_full, (((0,), (0,)), ((), ())), preferred_eleme...]
    unnamed x4 -> x7, local copies, waits for them, and re-layouts: 2.26 us -> 4.01 us
  transfers between devices with their start and end apart: 1 -> 0, of which waited for: 0 -> 0; matrix products, arithmetic and copies ran while one was open for 1% -> 0% of each run, Pallas kernels for 79% -> 0%
where the time goes in v2:
time: 70.3 us; the launch traced here: 70 us
  Pallas kernels  65 us (92%)
  local copies, waits for them, and re-layouts  4.91 us (7%)
    pallas_call x1, Pallas kernels, body(): pl.pallas_call(functools.partial(attention_kernel, n_head, n_ctx, n_part,...  65 us
    unnamed x7, local copies, waits for them, and re-layouts  4.01 us

profile of v2, /device:TPU:0, one launch (start us, length us, event | category | flops | bytes accessed | tf_op | source)
XLA Modules:
  0.0 70.0 jit_solution(5021431675767506898)
XLA Ops:
  0.0 0.9 %copy.6.gain_ref = f32[1024,1]{1,0:T(8,128)S(1)} copy(f32[1024,1]{0,1:T(1,128)} %bitcast.1) | data formatting | bytes 8192 | tf_op jit(solution)/shard_map/reshape | solution.py:385
  0.9 0.0 copy-start
  0.9 1.2 %copy-done = bf16[4,64,2048]{2,1,0:T(8,128)(2,1)S(1)} copy-done((bf16[4,64,2048]{2,1,0:T(8,128)(2,1)S(1)}, bf16[4,64,2048]{2,1,0:T(8,128)(2,1)}, u32[]{:S(2)}) %copy-start) | copy-done | bytes 1048600
  2.1 0.0 copy-start.1
  2.1 1.0 %copy-done.1 = bf16[256,1024]{1,0:T(8,128)(2,1)S(1)} copy-done((bf16[256,1024]{1,0:T(8,128)(2,1)S(1)}, bf16[256,1024]{1,0:T(8,128)(2,1)}, u32[]{:S(2)}) %copy-start.1) | copy-done | bytes 524312
  3.2 0.0 copy-start.2
  3.2 1.0 %copy-done.2 = bf16[256,1024]{1,0:T(8,128)(2,1)S(1)} copy-done((bf16[256,1024]{1,0:T(8,128)(2,1)S(1)}, bf16[256,1024]{1,0:T(8,128)(2,1)}, u32[]{:S(2)}) %copy-start.2) | copy-done | bytes 524312
  4.2 65.0 %shard_map.55 = bf16[128,1024]{1,0:T(8,128)(2,1)S(1)} custom-call(bf16[256,1024]{1,0:T(8,128)(2,1)S(1)} %copy-done.1, bf16[1024,2048]{1,0:T(8,128)(2,1)} %w_kv_ref.1, bf16[4,64,2048]{2,1,0:T(8,128)(2,1)S(1)} %copy-done, f32[1024,1]{1,0:T(8,128)S(1)} %copy.6.gain_ref, bf16[256,1024]{1,0:T(8,128)(2,1)S(1)} %copy-done.2), custom_call_target="tpu_custom_call" | custom-call | flops 3221225472 | bytes 5767168 | tf_op jit(solution)/shard_map/pallas_call | solution.py:343
  69.3 0.7 %copy.8 = bf16[128,1024]{1,0:T(8,128)(2,1)} copy(bf16[128,1024]{1,0:T(8,128)(2,1)S(1)} %shard_map.55) | data formatting | bytes 524288
Async XLA Ops:
  0.9 1.2 %copy-start = (bf16[4,64,2048]{2,1,0:T(8,128)(2,1)S(1)}, bf16[4,64,2048]{2,1,0:T(8,128)(2,1)}, u32[]{:S(2)}) copy-start(bf16[4,64,2048]{2,1,0:T(8,128)(2,1)} %queries_ref.1) | copy-start | bytes 3145732
  2.1 1.0 %copy-start.1 = (bf16[256,1024]{1,0:T(8,128)(2,1)S(1)}, bf16[256,1024]{1,0:T(8,128)(2,1)}, u32[]{:S(2)}) copy-start(bf16[256,1024]{1,0:T(8,128)(2,1)} %context_ref.1) | copy-start | bytes 1572868
  3.2 1.0 %copy-start.2 = (bf16[256,1024]{1,0:T(8,128)(2,1)S(1)}, bf16[256,1024]{1,0:T(8,128)(2,1)}, u32[]{:S(2)}) copy-start(bf16[256,1024]{1,0:T(8,128)(2,1)} %w_out_ref.1) | copy-start | bytes 1572868

commit v3 on v2

--- a/solution.py
+++ b/solution.py
@@ -82,20 +82,16 @@
         for copy in w_pending[key]:
             copy.wait_recv()
 
-    head_levels = list(reversed(range(n_head.bit_length() - 1)))
     part_levels = list(reversed(range(n_part.bit_length() - 1)))
-    w_masks = {"head": [0], "part": [0]}
+    part_masks = [0]
 
     def w_head(level):
-        bit = 1 << level
-        for mask in w_masks["head"]:
-            index = (mask | bit) - 1
-            block = w_all.at[0, my_head ^ mask]
+        for mask in range(n_head - 1, 0, -1):
+            block = w_all.at[0, my_head]
             send_w(
                 ("head", level), block, block,
-                wh_ssem.at[index], wh_rsem.at[index], {"head": my_head ^ bit},
-            )
-        w_masks["head"] += [mask | bit for mask in w_masks["head"]]
+                wh_ssem.at[mask - 1], wh_rsem.at[mask - 1], {"head": my_head ^ mask},
+            )
 
     def w_part(level):
         bit = 1 << level
@@ -103,15 +99,15 @@
             where = {"groups": my_group ^ (bit // ctx_parts)}
         else:
             where = {"ctx": my_ctx ^ bit}
-        for mask in w_masks["part"]:
+        for mask in part_masks:
             index = (mask | bit) - 1
             send_w(
                 ("part", level), w_all.at[mask], w_all.at[mask | bit],
                 wp_ssem.at[index], wp_rsem.at[index], where,
             )
-        w_masks["part"] += [mask | bit for mask in w_masks["part"]]
-
-    w_steps = [("head", level) for level in head_levels]
+        part_masks.extend([mask | bit for mask in part_masks])
+
+    w_steps = [("head", 0)]
     w_steps += [("part", level) for level in part_levels]
     w_done = [0]
 
@@ -289,7 +285,8 @@
 
     for step in range(heads_local + n_stage):
         if step < heads_local:
-            advance_w()
+            if step % 2 == 0:
+                advance_w()
             for mask in far:
                 kv_copies[mask, step].wait_recv()
                 attend(mask, step, False)

time: 70.3 us -> 66.6 us (0.947)
  Pallas kernels: 65 us -> 61.4 us
    pallas_call x1, Pallas kernels: 65 us -> 61.4 us  [body(): pl.pallas_call(functools.partial(attention_kernel, n_head, n_ctx, n_part,...]
where the time goes in v3:
time: 66.6 us; the launch traced here: 66.3 us
  Pallas kernels  61.4 us (92%)
  local copies, waits for them, and re-layouts  4.91 us (7%)
    pallas_call x1, Pallas kernels, body(): pl.pallas_call(functools.partial(attention_kernel, n_head, n_ctx, n_part,...  61.4 us
    unnamed x7, local copies, waits for them, and re-layouts  4.01 us

profile of v3, /device:TPU:0, one launch (start us, length us, event | category | flops | bytes accessed | tf_op | source)
XLA Modules:
  0.0 66.3 jit_solution(2039504169593721835)
XLA Ops:
  0.0 0.9 %copy.6.gain_ref = f32[1024,1]{1,0:T(8,128)S(1)} copy(f32[1024,1]{0,1:T(1,128)} %bitcast.1) | data formatting | bytes 8192 | tf_op jit(solution)/shard_map/reshape | solution.py:382
  0.9 0.0 copy-start
  0.9 1.2 %copy-done = bf16[4,64,2048]{2,1,0:T(8,128)(2,1)S(1)} copy-done((bf16[4,64,2048]{2,1,0:T(8,128)(2,1)S(1)}, bf16[4,64,2048]{2,1,0:T(8,128)(2,1)}, u32[]{:S(2)}) %copy-start) | copy-done | bytes 1048600
  2.1 0.0 copy-start.1
  2.1 1.0 %copy-done.1 = bf16[256,1024]{1,0:T(8,128)(2,1)S(1)} copy-done((bf16[256,1024]{1,0:T(8,128)(2,1)S(1)}, bf16[256,1024]{1,0:T(8,128)(2,1)}, u32[]{:S(2)}) %copy-start.1) | copy-done | bytes 524312
  3.2 0.0 copy-start.2
  3.2 1.0 %copy-done.2 = bf16[256,1024]{1,0:T(8,128)(2,1)S(1)} copy-done((bf16[256,1024]{1,0:T(8,128)(2,1)S(1)}, bf16[256,1024]{1,0:T(8,128)(2,1)}, u32[]{:S(2)}) %copy-start.2) | copy-done | bytes 524312
  4.2 61.4 %shard_map.55 = bf16[128,1024]{1,0:T(8,128)(2,1)S(1)} custom-call(bf16[256,1024]{1,0:T(8,128)(2,1)S(1)} %copy-done.1, bf16[1024,2048]{1,0:T(8,128)(2,1)} %w_kv_ref.1, bf16[4,64,2048]{2,1,0:T(8,128)(2,1)S(1)} %copy-done, f32[1024,1]{1,0:T(8,128)S(1)} %copy.6.gain_ref, bf16[256,1024]{1,0:T(8,128)(2,1)S(1)} %copy-done.2), custom_call_target="tpu_custom_call" | custom-call | flops 3221225472 | bytes 5767168 | tf_op jit(solution)/shard_map/pallas_call | solution.py:340
  65.6 0.7 %copy.8 = bf16[128,1024]{1,0:T(8,128)(2,1)} copy(bf16[128,1024]{1,0:T(8,128)(2,1)S(1)} %shard_map.55) | data formatting | bytes 524288
Async XLA Ops:
  0.9 1.2 %copy-start = (bf16[4,64,2048]{2,1,0:T(8,128)(2,1)S(1)}, bf16[4,64,2048]{2,1,0:T(8,128)(2,1)}, u32[]{:S(2)}) copy-start(bf16[4,64,2048]{2,1,0:T(8,128)(2,1)} %queries_ref.1) | copy-start | bytes 3145732
  2.1 1.0 %copy-start.1 = (bf16[256,1024]{1,0:T(8,128)(2,1)S(1)}, bf16[256,1024]{1,0:T(8,128)(2,1)}, u32[]{:S(2)}) copy-start(bf16[256,1024]{1,0:T(8,128)(2,1)} %context_ref.1) | copy-start | bytes 1572868
  3.2 1.0 %copy-start.2 = (bf16[256,1024]{1,0:T(8,128)(2,1)S(1)}, bf16[256,1024]{1,0:T(8,128)(2,1)}, u32[]{:S(2)}) copy-start(bf16[256,1024]{1,0:T(8,128)(2,1)} %w_out_ref.1) | copy-start | bytes 1572868

commit v4 on v3

--- a/solution.py
+++ b/solution.py
@@ -150,13 +150,12 @@
         if len(far) > 1 and mask == far[0]:
             send_kv(mask, 0)
         elif far and mask == far[-1]:
+            send_kv(mask, 0)
+        elif mask == 1:
             for head in range(heads_local):
-                for other in far:
+                for other in far + near:
                     if (other, head) not in kv_copies:
                         send_kv(other, head)
-        elif mask == 1:
-            for head in range(heads_local):
-                send_kv(1, head)
     project_into(0, kv_all)
 
     def attend(slot, head, first):
@@ -186,17 +185,12 @@
             total[head, :, span] = row_total
             acc[head, :, span] = summed
 
-    for slot in [0] + near:
-        if slot:
-            advance_w()
-            for head in range(heads_local):
-                kv_copies[slot, head].wait_recv()
-
-        def one_head(head, carry, slot=slot):
-            attend(slot, head, slot == 0)
-            return carry
-
-        lax.fori_loop(0, heads_local, one_head, 0)
+    def one_head(head, carry):
+        attend(0, head, True)
+        return carry
+
+    lax.fori_loop(0, heads_local, one_head, 0)
+    advance_w()
 
     copies = []
     pending = {}
@@ -285,9 +279,9 @@
 
     for step in range(heads_local + n_stage):
         if step < heads_local:
-            if step % 2 == 0:
+            if step:
                 advance_w()
-            for mask in far:
+            for mask in near + far:
                 kv_copies[mask, step].wait_recv()
                 attend(mask, step, False)
             send_stage(step, 0)
@@ -338,7 +332,7 @@
     dma = pltpu.SemaphoreType.DMA
     vmem = pl.BlockSpec(memory_space=pltpu.VMEM)
     return pl.pallas_call(
-        functools.partial(attention_kernel, n_head, n_ctx, n_part, min(1024, latents)),
+        functools.partial(attention_kernel, n_head, n_ctx, n_part, min(2048, latents)),
         out_shape=jax.ShapeDtypeStruct((own_rows, model_width), jnp.bfloat16),
         in_specs=[vmem] * 5,
         out_specs=vmem,

time: 66.6 us -> 61 us (0.916)
  Pallas kernels: 61.4 us -> 55.7 us
    pallas_call x1, Pallas kernels: 61.4 us -> 55.7 us  [body(): pl.pallas_call(functools.partial(attention_kernel, n_head, n_ctx, n_part,...]
where the time goes in v4:
time: 61 us; the launch traced here: 60.7 us
  Pallas kernels  55.7 us (91%)
  local copies, waits for them, and re-layouts  4.91 us (8%)
    pallas_call x1, Pallas kernels, body(): pl.pallas_call(functools.partial(attention_kernel, n_head, n_ctx, n_part,...  55.7 us
    unnamed x7, local copies, waits for them, and re-layouts  4.01 us

profile of v4, /device:TPU:0, one launch (start us, length us, event | category | flops | bytes accessed | tf_op | source)
XLA Modules:
  0.0 60.7 jit_solution(5470717687966934904)
XLA Ops:
  0.0 0.9 %copy.6.gain_ref = f32[1024,1]{1,0:T(8,128)S(1)} copy(f32[1024,1]{0,1:T(1,128)} %bitcast.1) | data formatting | bytes 8192 | tf_op jit(solution)/shard_map/reshape | solution.py:376
  0.9 0.0 copy-start
  0.9 1.2 %copy-done = bf16[4,64,2048]{2,1,0:T(8,128)(2,1)S(1)} copy-done((bf16[4,64,2048]{2,1,0:T(8,128)(2,1)S(1)}, bf16[4,64,2048]{2,1,0:T(8,128)(2,1)}, u32[]{:S(2)}) %copy-start) | copy-done | bytes 1048600
  2.1 0.0 copy-start.1
  2.1 1.0 %copy-done.1 = bf16[256,1024]{1,0:T(8,128)(2,1)S(1)} copy-done((bf16[256,1024]{1,0:T(8,128)(2,1)S(1)}, bf16[256,1024]{1,0:T(8,128)(2,1)}, u32[]{:S(2)}) %copy-start.1) | copy-done | bytes 524312
  3.2 0.0 copy-start.2
  3.2 1.0 %copy-done.2 = bf16[256,1024]{1,0:T(8,128)(2,1)S(1)} copy-done((bf16[256,1024]{1,0:T(8,128)(2,1)S(1)}, bf16[256,1024]{1,0:T(8,128)(2,1)}, u32[]{:S(2)}) %copy-start.2) | copy-done | bytes 524312
  4.2 55.7 %shard_map.55 = bf16[128,1024]{1,0:T(8,128)(2,1)S(1)} custom-call(bf16[256,1024]{1,0:T(8,128)(2,1)S(1)} %copy-done.1, bf16[1024,2048]{1,0:T(8,128)(2,1)} %w_kv_ref.1, bf16[4,64,2048]{2,1,0:T(8,128)(2,1)S(1)} %copy-done, f32[1024,1]{1,0:T(8,128)S(1)} %copy.6.gain_ref, bf16[256,1024]{1,0:T(8,128)(2,1)S(1)} %copy-done.2), custom_call_target="tpu_custom_call" | custom-call | flops 3221225472 | bytes 5767168 | tf_op jit(solution)/shard_map/pallas_call | solution.py:334
  60.0 0.7 %copy.8 = bf16[128,1024]{1,0:T(8,128)(2,1)} copy(bf16[128,1024]{1,0:T(8,128)(2,1)S(1)} %shard_map.55) | data formatting | bytes 524288
Async XLA Ops:
  0.9 1.2 %copy-start = (bf16[4,64,2048]{2,1,0:T(8,128)(2,1)S(1)}, bf16[4,64,2048]{2,1,0:T(8,128)(2,1)}, u32[]{:S(2)}) copy-start(bf16[4,64,2048]{2,1,0:T(8,128)(2,1)} %queries_ref.1) | copy-start | bytes 3145732
  2.1 1.0 %copy-start.1 = (bf16[256,1024]{1,0:T(8,128)(2,1)S(1)}, bf16[256,1024]{1,0:T(8,128)(2,1)}, u32[]{:S(2)}) copy-start(bf16[256,1024]{1,0:T(8,128)(2,1)} %context_ref.1) | copy-start | bytes 1572868
  3.2 1.0 %copy-start.2 = (bf16[256,1024]{1,0:T(8,128)(2,1)S(1)}, bf16[256,1024]{1,0:T(8,128)(2,1)}, u32[]{:S(2)}) copy-start(bf16[256,1024]{1,0:T(8,128)(2,1)} %w_out_ref.1) | copy-start | bytes 1572868
